TPU v7x, 32 devices: a whole 2x2x4 slice. The times are simulated.
32 devices in a mesh: groups: 2 (over y), ha: 4 (over z), ta: 2 (over x), col: 2 (over core).
Axes of the slice: x: 2, y: 2, z: 4, core: 2. Of those that a mesh axis runs over, the one named last changes fastest.
Arguments:
- tokens: bfloat16 [8, 16, 64, 768], P(('groups', 'ta'), 'ha', None, 'col'), parts along dimension 0, may hold values from -6 to 6
- norm1_gain: float32 [768], replicated, may hold values from 0.4 to 1.6
- w_qkv: bfloat16 [3, 768, 768], P(None, None, 'col'), may hold values from -0.21875 to 0.21875
- w_out: bfloat16 [768, 768], P('col'), may hold values from -0.3125 to 0.3125
- norm2_gain: float32 [768], replicated, may hold values from 0.4 to 1.6
- w_up: bfloat16 [768, 3072], P('ha', 'col'), may hold values from -0.21875 to 0.21875
- w_down: bfloat16 [3072, 768], P('col', 'ha'), may hold values from -0.109375 to 0.109375
Outputs:
- block_out: bfloat16 [8, 16, 64, 768], P(('groups', 'ta'), 'ha', None, 'col'), parts along dimension 0
There are 2 independent parts, one for each index of `groups`. A program takes and returns all parts, laid end to end along the dimension named above; an argument that names none is the same for every part. Nothing has to cross between parts.
All inputs are finite; a program needn't handle non-finite values.
Results may differ from a plain program's by a relative error of at most 0.009.
Values may be sent and summed in bfloat16 or wider, within the bound.
A program may use at most 64 MiB of HBM per device.

v0:
```python
import math

import jax
import jax.numpy as jnp
from jax import lax
from jax.sharding import PartitionSpec as P

HD = 64


EPS = 1e-05


def layer_norm(values, gain):
    mean = jnp.mean(values, -1, keepdims=True)
    centred = values - mean
    spread = jnp.mean(centred * centred, -1, keepdims=True)
    return centred * lax.rsqrt(spread + EPS) * gain


def attend(query, keys, values, dim):
    scale = 1.0 / math.sqrt(HD)
    moved_q = jnp.moveaxis(query, dim, -2)
    moved_k = jnp.moveaxis(keys, dim, -2)
    moved_v = jnp.moveaxis(values, dim, -2)
    shape = moved_q.shape
    split = shape[:-1] + (shape[-1] // HD, HD)
    scores = (
        jnp.einsum(
            "...qhd,...khd->...hqk",
            moved_q.reshape(split),
            moved_k.reshape(split),
            preferred_element_type=jnp.float32,
        )
        * scale
    )
    weights = jnp.exp(scores)
    weights = (weights / jnp.sum(weights, -1, keepdims=True)).astype(jnp.bfloat16)
    result = jnp.einsum(
        "...hqk,...khd->...qhd", weights, moved_v.reshape(split), preferred_element_type=jnp.float32
    ).astype(jnp.bfloat16)
    return jnp.moveaxis(result.reshape(shape), -2, dim)


def on_device(tokens, norm1_gain, w_qkv, w_out, norm2_gain, w_up, w_down):
    whole = lax.all_gather(tokens, "col", axis=3, tiled=True)
    frames, rows_h, width, model = whole.shape
    count = frames * rows_h * width
    half = tokens.shape[3]
    wide = whole.astype(jnp.float32).reshape(count, model)
    normed = layer_norm(wide, norm1_gain).astype(jnp.bfloat16)
    stacked = jnp.einsum("rd,sdc->src", normed, w_qkv, preferred_element_type=jnp.float32).astype(
        jnp.bfloat16
    )
    stacked = stacked.reshape(3, frames, rows_h, width, half)
    along_w = attend(stacked[0], stacked[1], stacked[2], 2)
    columns = lax.all_to_all(stacked, "ha", split_axis=3, concat_axis=2, tiled=True)
    along_h_far = attend(columns[0], columns[1], columns[2], 1)
    along_h = lax.all_to_all(along_h_far, "ha", split_axis=1, concat_axis=2, tiled=True)
    lines = lax.all_to_all(stacked, "ta", split_axis=3, concat_axis=1, tiled=True)
    along_t_far = attend(lines[0], lines[1], lines[2], 0)
    along_t = lax.all_to_all(along_t_far, "ta", split_axis=0, concat_axis=2, tiled=True)
    mixed = (
        along_w.astype(jnp.float32) + along_h.astype(jnp.float32) + along_t.astype(jnp.float32)
    ).astype(jnp.bfloat16)
    terms = jnp.dot(mixed.reshape(count, half), w_out, preferred_element_type=jnp.float32)
    offset = lax.axis_index("col") * half
    summed = lax.psum(terms, "col")
    first_full = wide + summed
    second = layer_norm(first_full, norm2_gain).astype(jnp.bfloat16)
    first = lax.dynamic_slice_in_dim(first_full, offset, half, 1)
    upper = jnp.dot(
        second, lax.all_gather(w_up, "ha", axis=0, tiled=True), preferred_element_type=jnp.float32
    )
    hidden = jax.nn.gelu(upper, approximate=False).astype(jnp.bfloat16)
    down_terms = jnp.dot(
        hidden, lax.all_gather(w_down, "ha", axis=1, tiled=True), preferred_element_type=jnp.float32
    )
    down_share = lax.psum_scatter(
        down_terms.astype(jnp.bfloat16), "col", scatter_dimension=1, tiled=True
    ).astype(jnp.float32)
    return (first + down_share).astype(jnp.bfloat16).reshape(frames, rows_h, width, half)


def solution(mesh):
    placed = (
        P(("groups", "ta"), "ha", None, "col"),
        P(),
        P(None, None, "col"),
        P("col", None),
        P(),
        P("ha", "col"),
        P("col", "ha"),
    )
    return jax.shard_map(
        on_device,
        mesh=mesh,
        in_specs=placed,
        out_specs=P(("groups", "ta"), "ha", None, "col"),
        check_vma=False,
    )
```

profile of v0, /device:TPU:0, one launch (start us, length us, event | category | flops | bytes accessed | tf_op | source)
XLA Modules:
  0.0 270.8 jit_solution(178408443112723178)
XLA Ops:
  7.4 2.8 %all_gather.9 = bf16[2,4,64,768]{3,2,1,0:T(8,128)(2,1)S(1)} all-gather(bf16[2,4,64,384]{3,2,1,0:T(8,128)(2,1)} %param.7), channel_id=1, replica_groups=mesh['groups'=2,'ha'=4,'ta'=2,'col'=2] {'col'}, dimensions={3}, use_global_device_ids=true | all-gather | bytes 1179648 | tf_op jit(solution)/shard_map/all_gather | solution.py:46
  10.3 0.3 fusion.11
  11.2 1.2 convolution_convert_fusion
  12.4 1.0 copy-done.4
  13.4 0.9 copy.127
  14.4 1.0 copy-done.1
  15.4 19.9 %all_to_all.48 = bf16[3,2,4,64,384]{4,2,1,0,3:T(4,128)(2,1)} all-to-all(bf16[3,2,4,64,384]{4,2,1,0,3:T(4,128)(2,1)S(1)} %copy.127), channel_id=1, replica_groups=mesh['groups'=2,'ha'=4,'ta'=2,'col'=2] {'ta'}, dimensions={3} | all-to-all | bytes 2359296 | tf_op jit(solution)/shard_map/all_to_all | solution.py:60
  35.3 5.1 %all-to-all-start = ((bf16[3,2,4,64,384]{4,2,1,0,3:T(4,128)(2,1)}), bf16[3,2,4,64,384]{4,2,1,0,3:T(4,128)(2,1)}, u32[]{:S(2)}, u32[]{:S(2)}) async-start(bf16[3,2,4,64,384]{4,2,1,0,3:T(4,128)(2,1)} %copy-done.1), calls=%async_computation | async-start | bytes 2359296 | tf_op jit(solution)/shard_map/all_to_all | solution.py:57
  40.4 2.1 fusion.92
  42.5 2.4 reshape.133
  44.9 1.5 reshape.134
  46.5 1.5 copy.145
  47.9 0.9 fusion.93
  48.8 0.8 copy.148
  49.6 2.4 reshape.139
  52.0 1.8 copy.150
  53.8 2.4 reshape.140
  56.2 3.9 %fusion.23 = f32[4,32,6,4,4]{3,4,2,1,0:T(4,128)} fusion(bf16[4,32,4,6,64]{4,3,1,0,2:T(8,128)(2,1)} %reshape.140, bf16[4,32,4,6,64]{4,3,1,0,2:T(8,128)(2,1)} %reshape.139), kind=kOutput, calls=%fused_computation.46 | convolution fusion | flops 1572864 | bytes 835584 | tf_op jit(solution)/shard_map/...qhd,...khd->...hqk/dot_general | solution.py:29
  60.1 1.9 copy.154
  62.1 0.8 divide_convert_fusion.4
  62.9 2.3 copy.156
  65.2 0.8 copy.146
  66.0 2.4 reshape.138
  68.4 2.4 fusion.21
  70.8 1.2 copy.157
  72.0 1.9 reshape.124
  73.9 0.8 copy.158
  74.7 4.4 %all-to-all-start.3 = ((bf16[4,4,32,384]{3,2,1,0:T(8,128)(2,1)}), bf16[4,4,32,384]{3,2,1,0:T(8,128)(2,1)}, u32[]{:S(2)}, u32[]{:S(2)}) async-start(bf16[4,4,32,384]{3,2,1,0:T(8,128)(2,1)} %copy.158), calls=%async_computation.3 | async-start | bytes 786432 | tf_op jit(solution)/shard_map/all_to_all | solution.py:62
  79.1 1.5 copy.128
  80.5 0.9 fusion.91
  81.4 0.8 copy.131
  82.2 2.4 reshape.136
  84.6 1.8 copy.133
  86.4 2.4 reshape.137
  88.8 0.8 copy.129
  89.6 2.4 reshape.135
  92.1 3.8 %multiply_exponential_fusion = f32[2,16,6,16,16]{3,4,2,1,0:T(8,128)} fusion(bf16[2,16,16,6,64]{4,3,1,2,0:T(8,128)(2,1)} %reshape.137, bf16[2,16,16,6,64]{4,3,1,2,0:T(8,128)(2,1)} %reshape.136), kind=kOutput, calls=%fused_computation.32 | convolution fusion | flops 6340608 | bytes 983040 | tf_op jit(solution)/shard_map/...qhd,...khd->...hqk/dot_general | solution.py:29
  95.9 3.9 %fusion.20 = bf16[2,16,16,6,64]{4,2,3,1,0:T(8,128)(2,1)} fusion(f32[2,16,6,16,16]{3,4,2,1,0:T(8,128)} %multiply_exponential_fusion, bf16[2,16,16,6,64]{4,3,1,2,0:T(8,128)(2,1)} %reshape.135), kind=kOutput, calls=%fused_computation.41 | convolution fusion | flops 6589455 | bytes 983040 | tf_op jit(solution)/shard_map/...hqk,...khd->...qhd/dot_general | solution.py:39
  99.8 2.4 copy.139
  102.2 1.9 reshape.120
  104.0 0.8 copy.140
  104.9 5.1 %all-to-all-start.1 = ((bf16[2,16,16,384]{3,2,0,1:T(8,128)(2,1)}), bf16[2,16,16,384]{3,2,0,1:T(8,128)(2,1)}, u32[]{:S(2)}, u32[]{:S(2)}) async-start(bf16[2,16,16,384]{3,2,0,1:T(8,128)(2,1)} %copy.140), calls=%async_computation.1 | async-start | bytes 786432 | tf_op jit(solution)/shard_map/all_to_all | solution.py:59
  110.0 3.3 %multiply_exponential_fusion.1 = f32[2,4,6,64,64]{3,4,2,1,0:T(8,128)} fusion(bf16[2,4,64,6,64]{4,3,2,1,0:T(8,128)(2,1)} %reshape.134, bf16[2,4,64,6,64]{4,3,2,1,0:T(8,128)(2,1)} %reshape.133), kind=kOutput, calls=%fused_computation.34 | convolution fusion | flops 25362432 | bytes 1572864 | tf_op jit(solution)/shard_map/...qhd,...khd->...hqk/dot_general | solution.py:29
  113.2 1.5 reshape.132
  114.8 3.8 %convert_bitcast_fusion = f32[2,4,64,6,64]{2,4,3,1,0:T(8,128)} fusion(f32[2,4,6,64,64]{3,4,2,1,0:T(8,128)} %multiply_exponential_fusion.1, bf16[2,4,64,6,64]{4,3,2,1,0:T(8,128)(2,1)} %reshape.132), kind=kOutput, calls=%fused_computation.28 | convolution fusion | flops 25955392 | bytes 1966080 | tf_op jit(solution)/shard_map/...hqk,...khd->...qhd/dot_general | solution.py:39
  118.6 3.6 %copy.126 = f32[2,4,64,6,64]{2,1,0,4,3:T(4,128)} copy(f32[2,4,64,6,64]{2,4,3,1,0:T(8,128)} %convert_bitcast_fusion) | data formatting | bytes 1572864 | tf_op jit(solution)/shard_map/convert_element_type | solution.py:64
  122.2 3.1 %reshape.126 = f32[512,384]{0,1:T(8,128)} reshape(f32[2,4,64,6,64]{2,1,0,4,3:T(4,128)} %copy.126) | data formatting | bytes 1572864 | tf_op jit(solution)/shard_map/convert_element_type | solution.py:64
  125.4 1.1 convert_bitcast_fusion.1
  126.5 1.2 copy.160
  127.7 1.0 copy.141
  128.9 1.2 copy.143
  130.0 3.6 %fusion.44 = f32[512,768]{1,0:T(8,128)} fusion(bf16[384,768]{1,0:T(8,128)(2,1)} %param.10, f32[512,384]{0,1:T(8,128)} %copy.160, f32[512,384]{0,1:T(8,128)} %reshape.126, f32[512,384]{0,1:T(8,128)} %copy.143), kind=kOutput, calls=%fused_computation.64 | convolution fusion | flops 302579712 | bytes 4521984 | tf_op jit(solution)/shard_map/dot_general | solution.py:66
  133.7 0.5 all-gather.3.cloned.1.call-update
  134.3 0.5 all-gather.5.cloned.1.call-update
  135.1 20.9 %all-reduce.2.cloned.1.call-done = f32[512,768]{1,0:T(8,128)} async-done(((f32[512,768]{1,0:T(8,128)}), f32[512,768]{1,0:T(8,128)}) %all-reduce.2.cloned.1.call-update) | async-done | bytes 1572880 | tf_op jit(solution)/shard_map/psum | solution.py:68
  156.0 1.6 fusion.90
  157.7 1.1 copy-done.2
  159.1 28.4 %all-gather.3.cloned.1.call-done = bf16[768,1536]{1,0:T(8,128)(2,1)} async-done(((bf16[192,1536]{1,0:T(8,128)(2,1)}), bf16[768,1536]{1,0:T(8,128)(2,1)}) %all-gather.3.cloned.1.call-update) | async-done | bytes 2359312 | tf_op jit(solution)/shard_map/all_gather | solution.py:73
  187.6 50.3 %all-gather.5.cloned.1.call-done = bf16[1536,768]{0,1:T(8,128)(2,1)} async-done(((bf16[1536,192]{0,1:T(8,128)(2,1)}), bf16[1536,768]{0,1:T(8,128)(2,1)}) %all-gather.5.cloned.1.call-update) | async-done | bytes 2359312 | tf_op jit(solution)/shard_map/all_gather | solution.py:77
  237.8 12.3 %fusion.17 = bf16[512,768]{1,0:T(8,128)(2,1)} fusion(bf16[1536,768]{0,1:T(8,128)(2,1)} %all-gather.5.cloned.1.call-done, bf16[768,1536]{1,0:T(8,128)(2,1)} %all-gather.3.cloned.1.call-done, f32[512,768]{1,0:T(8,128)} %copy-done.2, f32[768]{0:T(1024)S(1)} %copy-done.6, f32[512]{0:T(512)S(1)} %add_rsqrt_fusion.1, f32[512]{0:T(512)S(1)} %broadcast_multiply_fusion.1), kind=kOutput, calls=%fused_computation.37 | convolution fusion | flops 2469003264 | bytes 7085056 | tf_op jit(solution)/shard_map/dot_general | solution.py:76
  250.1 2.4 copy.181
  252.6 7.0 %reduce-scatter.4.cloned.1.call-done = bf16[384,512]{1,0:T(8,128)(2,1)} async-done(((bf16[768,512]{1,0:T(8,128)(2,1)}), bf16[384,512]{1,0:T(8,128)(2,1)}) %reduce-scatter.4.cloned.1.call-update) | async-done | bytes 393232
  259.6 1.9 copy.182
  261.5 1.8 add_convert_fusion
  (33 shorter events, 1.8 us)
Async XLA Ops:
  7.4 3.8 %copy-start = (bf16[3,768,384]{2,1,0:T(8,128)(2,1)S(1)}, bf16[3,768,384]{2,1,0:T(8,128)(2,1)}, u32[]{:S(2)}) copy-start(bf16[3,768,384]{2,1,0:T(8,128)(2,1)} %param.9) | copy-start | bytes 5308420
  7.4 3.5 %copy-start.5 = (f32[768]{0:T(1024)S(1)}, f32[768]{0:T(1024)}, u32[]{:S(2)}) copy-start(f32[768]{0:T(1024)} %param.8) | copy-start | bytes 9220
  12.4 1.0 copy-start.4
  14.4 1.0 copy-start.1
  35.3 39.4 %all-to-all-start = ((bf16[3,2,4,64,384]{4,2,1,0,3:T(4,128)(2,1)}), bf16[3,2,4,64,384]{4,2,1,0,3:T(4,128)(2,1)}, u32[]{:S(2)}, u32[]{:S(2)}) async-start(bf16[3,2,4,64,384]{4,2,1,0,3:T(4,128)(2,1)} %copy-done.1), calls=%async_computation | async-start | bytes 2359296 | tf_op jit(solution)/shard_map/all_to_all | solution.py:57
  74.7 30.2 %all-to-all-start.3 = ((bf16[4,4,32,384]{3,2,1,0:T(8,128)(2,1)}), bf16[4,4,32,384]{3,2,1,0:T(8,128)(2,1)}, u32[]{:S(2)}, u32[]{:S(2)}) async-start(bf16[4,4,32,384]{3,2,1,0:T(8,128)(2,1)} %copy.158), calls=%async_computation.3 | async-start | bytes 786432 | tf_op jit(solution)/shard_map/all_to_all | solution.py:62
  104.9 22.8 %all-to-all-start.1 = ((bf16[2,16,16,384]{3,2,0,1:T(8,128)(2,1)}), bf16[2,16,16,384]{3,2,0,1:T(8,128)(2,1)}, u32[]{:S(2)}, u32[]{:S(2)}) async-start(bf16[2,16,16,384]{3,2,0,1:T(8,128)(2,1)} %copy.140), calls=%async_computation.1 | async-start | bytes 786432 | tf_op jit(solution)/shard_map/all_to_all | solution.py:59
  110.0 46.1 %all-reduce.2.cloned.1.call-start = ((), (), s32[]{:S(2)}) async-start(), calls=%async_computation.5 | async-start | bytes 3145728 | tf_op jit(solution)/shard_map/psum | solution.py:68
  133.7 53.9 %all-gather.3.cloned.1.call-start = ((), (), s32[]{:S(2)}) async-start(), calls=%async_computation.6 | async-start | bytes 2949120 | tf_op jit(solution)/shard_map/all_gather | solution.py:73
  134.2 103.6 %all-gather.5.cloned.1.call-start = ((), (), s32[]{:S(2)}) async-start(), calls=%async_computation.7 | async-start | bytes 2949120 | tf_op jit(solution)/shard_map/all_gather | solution.py:77
  134.8 103.0 %copy-start.6 = (f32[768]{0:T(1024)S(1)}, f32[768]{0:T(1024)}, u32[]{:S(2)}) copy-start(f32[768]{0:T(1024)} %param.11) | copy-start | bytes 9220
  134.8 124.8 %reduce-scatter.4.cloned.1.call-start = ((), (), s32[]{:S(2)}) async-start(), calls=%async_computation.8 | async-start | bytes 1179648
  157.7 1.2 copy-start.2
  250.1 11.4 %copy-start.3 = (f32[512,768]{1,0:T(8,128)S(1)}, f32[512,768]{1,0:T(8,128)}, u32[]{:S(2)}) copy-start(f32[512,768]{1,0:T(8,128)} %copy-done.2) | copy-start | bytes 4718596
Sparse Core Ops, SparseCore 0:
  133.8 22.2 all-reduce.1
  252.7 6.8 reduce-scatter.3
Sparse Core Ops, SparseCore 1:
  135.8 51.7 all-gather.2
  189.1 48.7 all-gather.4
where the time goes:
time: 272 us; the launch traced here: 271 us
  waiting for transfers between devices  108 us (40%)
  local copies, waits for them, and re-layouts  65.5 us (24%)
  matrix products  38.2 us (14%)
  blocking collectives  22.7 us (8%)
  between operations  15 us (6%)
  starting transfers between devices  14.9 us (5%)
  other arithmetic  6.71 us (2%)
    all_gather x1, waiting for transfers between devices, on_device(): lax.all_gather(w_down, 'ha', axis=1, tiled=True)  50.3 us
    all_gather x1, waiting for transfers between devices, on_device(): lax.all_gather(w_up, 'ha', axis=0, tiled=True)  28.4 us
    psum x1, waiting for transfers between devices, on_device(): summed = lax.psum(terms, 'col')  20.9 us
    all_to_all x1, blocking collectives, on_device(): lax.all_to_all(stacked, 'ta', split_axis=3, concat_axis=1, tiled=True)  19.9 us
    dot_general x1, matrix products, on_device(): jnp.dot(hidden, lax.all_gather(w_down, 'ha', axis=1, tiled=True), preferr...  12.3 us
    dot_general x3, matrix products, attend(): jnp.einsum('...qhd,...khd->...hqk', moved_q.reshape(split), moved_k.resha...  10.9 us
    dot_general x3, matrix products, attend(): jnp.einsum('...hqk,...khd->...qhd', weights, moved_v.reshape(split), pref...  10.2 us
    unnamed x5, waiting for transfers between devices  8.13 us
  transfers between devices with their start and end apart: 7, of which 4 were waited for; matrix products, arithmetic and copies ran while one was open for 29% of the time, Pallas kernels for 0%

commit v1 on v0

--- a/solution.py
+++ b/solution.py
@@ -1,8 +1,11 @@
+import functools
 import math
 
 import jax
 import jax.numpy as jnp
 from jax import lax
+from jax.experimental import pallas as pl
+from jax.experimental.pallas import tpu as pltpu
 from jax.sharding import PartitionSpec as P
 
 HD = 64
@@ -82,6 +85,369 @@
     return (first + down_share).astype(jnp.bfloat16).reshape(frames, rows_h, width, half)
 
 
+F32 = jnp.float32
+BF = jnp.bfloat16
+
+
+def norm_rows(parts, gain_ref, out_ref, rows):
+    half = parts[0].shape[-1]
+    model = 2 * half
+    total = jnp.sum(parts[0], -1, keepdims=True) + jnp.sum(parts[1], -1, keepdims=True)
+    mean = total * (1.0 / model)
+    centred = [part - mean for part in parts]
+    spread = sum(jnp.sum(part * part, -1, keepdims=True) for part in centred) * (1.0 / model)
+    factor = lax.rsqrt(spread + EPS)
+    for at, part in enumerate(centred):
+        gain = gain_ref[:, at * half : (at + 1) * half]
+        out_ref[rows, at * half : (at + 1) * half] = (part * factor * gain).astype(BF)
+
+
+def attend_pair(query, keys, values, mask):
+    count = query.shape[0]
+    low = lax.broadcasted_iota(jnp.int32, query.shape, 1) < HD
+    zero = jnp.zeros_like(query)
+    both = jnp.concatenate([jnp.where(low, query, zero), jnp.where(low, zero, query)], 0)
+    scores = lax.dot_general(both, keys, (((1,), (1,)), ((), ())), preferred_element_type=F32)
+    weights = jnp.where(mask, jnp.exp(scores), 0.0)
+    ones = jnp.ones((keys.shape[0], 128), BF)
+    sums = jnp.dot(weights.astype(BF), ones, preferred_element_type=F32)
+    probs = (weights / sums).astype(BF)
+    found = jnp.dot(probs, values, preferred_element_type=F32)
+    return jnp.where(low, found[:count], found[count:]).astype(BF).astype(F32)
+
+
+def block_kernel(
+    sizes, tok, gain1, wqkv_hbm, wout_hbm, gain2, wup_hbm, wdn_hbm, out,
+    own, sendb, strip, nrm, qkv, found, heads_w, backb, back, mix, first,
+    wq, wo, wu, wdl, wdp, wd, hid, downb, downr, wide,
+    sem_l, s_tok, r_tok, s_col, r_col, s_fwd, r_fwd, s_ret, r_ret,
+    s_z, r_z, s_p, r_p, s_mix, r_mix, s_dn, r_dn,
+):
+    n_g, n_ha, n_ta = sizes
+    g, z, t, c = (lax.axis_index(name) for name in ("groups", "ha", "ta", "col"))
+    oc = 1 - c
+    me = t * n_ha + z
+    half = tok.shape[2]
+    quarter = t * n_g + g
+    partner = {"col": oc}
+
+    def remote(src, dst, send, recv, to):
+        return pltpu.make_async_remote_copy(
+            src_ref=src, dst_ref=dst, send_sem=send, recv_sem=recv,
+            device_id=to, device_id_type=pl.DeviceIdType.MESH,
+        )
+
+    moves = [(dt, dz) for dt in range(n_ta) for dz in range(n_ha) if dt or dz]
+    plane = [(dt, dg) for dt in range(n_ta) for dg in range(n_g) if dt or dg]
+
+    def other(dt, dz):
+        return lax.rem(t + dt, n_ta), lax.rem(z + dz, n_ha)
+
+    barrier = pltpu.get_barrier_semaphore()
+    for dt, dz in moves:
+        to_t, to_z = other(dt, dz)
+        pl.semaphore_signal(barrier, inc=1, device_id={"ha": to_z, "ta": to_t}, device_id_type=pl.DeviceIdType.MESH)
+    pl.semaphore_signal(barrier, inc=1, device_id=partner, device_id_type=pl.DeviceIdType.MESH)
+    for dt, dg in plane:
+        if dg:
+            to = {"groups": lax.rem(g + dg, n_g), "ta": lax.rem(t + dt, n_ta)}
+            pl.semaphore_signal(barrier, inc=1, device_id=to, device_id_type=pl.DeviceIdType.MESH)
+
+    local = [
+        pltpu.make_async_copy(wdn_hbm, wdl, sem_l.at[0]),
+        pltpu.make_async_copy(wqkv_hbm, wq, sem_l.at[1]),
+        pltpu.make_async_copy(wout_hbm, wo.at[c], sem_l.at[2]),
+        pltpu.make_async_copy(wup_hbm, wu.at[z], sem_l.at[3]),
+    ]
+    for copy in local:
+        copy.start()
+
+    lines = tok.shape[0]
+    tokens = tok[...].astype(F32)
+    narrow = tok.shape[1] // (n_ha * n_ta)
+    for s in range(n_ha * n_ta):
+        cut = tokens[:, s * narrow : (s + 1) * narrow, :]
+        sendb[s] = cut.reshape(lines * narrow, half).astype(BF)
+    own[c] = tok[...]
+    strip[c, me] = sendb[me]
+
+    n_sig = len(moves) + 1 + sum(1 for dt, dg in plane if dg)
+    pl.semaphore_wait(barrier, n_sig)
+
+    own_send = remote(own.at[c], own.at[c], s_col.at[0], r_col.at[0], partner)
+    own_send.start()
+    sends = []
+    for at, (dt, dz) in enumerate(moves):
+        to_t, to_z = other(dt, dz)
+        copy = remote(sendb.at[to_t * n_ha + to_z], strip.at[c, me], s_tok.at[at], r_tok.at[at], {"ha": to_z, "ta": to_t})
+        copy.start()
+        sends.append(copy)
+    forward = remote(strip.at[c, me], strip.at[c, me], s_fwd.at[len(moves)], r_fwd.at[len(moves)], partner)
+    forward.start()
+    sends.append(forward)
+
+    z_up, z_down = [], []
+    local[0].wait()
+    part_rows = wdl.shape[0] // 4
+    for q in range(4):
+        piece = wdl[q * part_rows : (q + 1) * part_rows, :].astype(F32)
+        wdp[z, q, :part_rows] = piece[:, :128].astype(BF)
+        rest = piece[:, 128:]
+        wdp[z, q, part_rows:] = jnp.concatenate([rest[: part_rows // 2], rest[part_rows // 2 :]], 1).astype(BF)
+    for d in range(1, n_ha):
+        to = {"ha": lax.rem(z + d, n_ha)}
+        copy = remote(wup_hbm.at[quarter], wu.at[z, quarter], s_z.at[0, d], r_z.at[0, d], to)
+        copy.start()
+        z_up.append(copy)
+    for d in range(1, n_ha):
+        to = {"ha": lax.rem(z + d, n_ha)}
+        copy = remote(wdp.at[z, quarter], wdp.at[z, quarter], s_z.at[1, d], r_z.at[1, d], to)
+        copy.start()
+        z_down.append(copy)
+    local[1].wait()
+    local[2].wait()
+    wo_send = remote(wo.at[c], wo.at[c], s_col.at[1], r_col.at[1], partner)
+    wo_send.start()
+    sends += z_up + z_down
+
+    def project():
+        for i in range(3):
+            value = jnp.dot(nrm[...], wq[i], preferred_element_type=F32)
+            if i == 0:
+                value = value.astype(BF).astype(F32) * (1.0 / math.sqrt(HD))
+            qkv[i] = value.astype(BF).reshape(qkv.shape[1:])
+
+    count = lines * tok.shape[1]
+    block = 128
+    rows_at = lax.rem(lax.broadcasted_iota(jnp.int32, (2 * block, block), 0), block)
+    cols_at = lax.broadcasted_iota(jnp.int32, (2 * block, block), 1)
+    pairs = half // 128
+
+    own_send.wait()
+    norm_rows(
+        [own[0].reshape(count, half).astype(F32), own[1].reshape(count, half).astype(F32)],
+        gain1, nrm, slice(None),
+    )
+    project()
+    width = tok.shape[1]
+    mask_w = rows_at // width == cols_at // width
+    flat = qkv.reshape(3, count // block, block, half)
+
+    def along_w(b, carry):
+        for p in range(pairs):
+            lanes = pl.ds(p * 128, 128)
+            heads_w[b, :, lanes] = attend_pair(flat[0, b, :, lanes], flat[1, b, :, lanes], flat[2, b, :, lanes], mask_w)
+        return carry
+
+    lax.fori_loop(0, count // block, along_w, 0)
+
+    for at, (dt, dz) in enumerate(moves):
+        from_t, from_z = lax.rem(t + n_ta - dt, n_ta), lax.rem(z + n_ha - dz, n_ha)
+        src = from_t * n_ha + from_z
+        remote(sendb.at[0], strip.at[c, src], s_tok.at[at], r_tok.at[at], partner).wait_recv()
+        copy = remote(strip.at[c, src], strip.at[c, src], s_fwd.at[at], r_fwd.at[at], partner)
+        copy.start()
+        sends.append(copy)
+    for at, (dt, dz) in enumerate(moves + [(0, 0)]):
+        from_t, from_z = lax.rem(t + n_ta - dt, n_ta), lax.rem(z + n_ha - dz, n_ha)
+        src = from_t * n_ha + from_z
+        remote(strip.at[oc, src], strip.at[oc, src], s_fwd.at[at], r_fwd.at[at], partner).wait_recv()
+    norm_rows(
+        [strip[0].reshape(count, half).astype(F32), strip[1].reshape(count, half).astype(F32)],
+        gain1, nrm, slice(None),
+    )
+    project()
+    frames = 2
+    mask_h = lax.rem(rows_at, narrow) == lax.rem(cols_at, narrow)
+    same = lines // frames * narrow
+    mask_t = lax.rem(rows_at, same) == lax.rem(cols_at, same)
+
+    def along_h(b, carry):
+        tt, ff = b // frames, lax.rem(b, frames)
+        for p in range(pairs):
+            lanes = pl.ds(p * 128, 128)
+            q, k, v = (qkv[i, tt, :, ff, :, lanes].reshape(block, 128) for i in range(3))
+            found[tt, :, ff, :, lanes] = attend_pair(q, k, v, mask_h).reshape(n_ha, same, 128)
+        return carry
+
+    def along_t(zz, carry):
+        for p in range(pairs):
+            lanes = pl.ds(p * 128, 128)
+            q, k, v = (qkv[i, :, zz, :, :, lanes].reshape(block, 128) for i in range(3))
+            more = attend_pair(q, k, v, mask_t).reshape(n_ta, frames, same, 128)
+            backb[:, zz, :, :, lanes] = (found[:, zz, :, :, lanes] + more).astype(BF)
+        return carry
+
+    lax.fori_loop(0, n_ta * frames, along_h, 0)
+    lax.fori_loop(0, n_ha, along_t, 0)
+
+    for at, (dt, dz) in enumerate(moves):
+        to_t, to_z = other(dt, dz)
+        copy = remote(backb.at[to_t, to_z], back.at[t, z], s_ret.at[at], r_ret.at[at], {"ha": to_z, "ta": to_t})
+        copy.start()
+        sends.append(copy)
+    back[t, z] = backb[t, z]
+
+    def spread(kind, buf):
+        for d in range(1, n_ha):
+            zz = lax.rem(z + n_ha - d, n_ha)
+            remote(buf.at[zz, quarter], buf.at[zz, quarter], s_z.at[kind, d], r_z.at[kind, d], partner).wait_recv()
+            for at, (dt, dg) in enumerate(plane):
+                to = {"groups": lax.rem(g + dg, n_g), "ta": lax.rem(t + dt, n_ta)}
+                copy = remote(buf.at[zz, quarter], buf.at[zz, quarter], s_p.at[kind, d, at], r_p.at[kind, d, at], to)
+                copy.start()
+                sends.append(copy)
+
+    def spread_wait(kind, buf):
+        for d in range(1, n_ha):
+            zz = lax.rem(z + n_ha - d, n_ha)
+            for at, (dt, dg) in enumerate(plane):
+                qq = lax.rem(t + n_ta - dt, n_ta) * n_g + lax.rem(g + n_g - dg, n_g)
+                remote(buf.at[zz, qq], buf.at[zz, qq], s_p.at[kind, d, at], r_p.at[kind, d, at], partner).wait_recv()
+
+    spread(0, wu)
+
+    for at, (dt, dz) in enumerate(moves):
+        from_t, from_z = lax.rem(t + n_ta - dt, n_ta), lax.rem(z + n_ha - dz, n_ha)
+        remote(back.at[from_t, from_z], back.at[from_t, from_z], s_ret.at[at], r_ret.at[at], partner).wait_recv()
+    for s in range(n_ha * n_ta):
+        piece = back[s // n_ha, s % n_ha].astype(F32)
+        wide[:, s * narrow : (s + 1) * narrow, :] = piece.reshape(lines, narrow, half)
+    mix[c] = (wide[...].reshape(count, half) + heads_w[...].reshape(count, half)).astype(BF)
+    mix_send = remote(mix.at[c], mix.at[c], s_mix.at[0], r_mix.at[0], partner)
+    mix_send.start()
+    spread(1, wdp)
+    wo_send.wait()
+    first[...] = jnp.dot(mix[c], wo[c], preferred_element_type=F32)
+    mix_send.wait()
+    first[...] += jnp.dot(mix[oc], wo[oc], preferred_element_type=F32)
+    parts = []
+    for i in range(2):
+        cols = slice(i * half, (i + 1) * half)
+        part = own[i].reshape(count, half).astype(F32) + first[:, cols]
+        first[:, cols] = part
+        parts.append(part)
+    norm_rows(parts, gain2, nrm, slice(None))
+
+    local[3].wait()
+    spread_wait(0, wu)
+    units = wu.shape[3]
+    step = 256
+
+    def feed(u, carry):
+        cols = pl.ds(pl.multiple_of(u * step, step), step)
+        up = jnp.dot(nrm[...], wu[:, :, :, cols].reshape(2 * half, step), preferred_element_type=F32)
+        up = 0.5 * up * (1.0 + lax.erf(up * math.sqrt(0.5)))
+        hid[:, cols] = up.astype(BF)
+        return carry
+
+    lax.fori_loop(0, units // step, feed, 0)
+
+    spread_wait(1, wdp)
+    small = part_rows // 2
+    low = lax.broadcasted_iota(jnp.int32, (small, 128), 1) < 64
+    for q in range(4):
+        for zp in range(n_ha // 2):
+            lead = zp * 384
+            rows = slice(q * part_rows, (q + 1) * part_rows)
+            wd[rows, lead : lead + 128] = wdp[2 * zp, q, :part_rows]
+            wd[rows, lead + 128 : lead + 256] = wdp[2 * zp + 1, q, :part_rows]
+            even = wdp[2 * zp, q, part_rows:].astype(F32)
+            odd = wdp[2 * zp + 1, q, part_rows:].astype(F32)
+            wd[q * part_rows : q * part_rows + small, lead + 256 : lead + 384] = jnp.where(low, even, pltpu.roll(odd, 64, 1)).astype(BF)
+            wd[q * part_rows + small : (q + 1) * part_rows, lead + 256 : lead + 384] = jnp.where(low, pltpu.roll(even, 64, 1), odd).astype(BF)
+
+    there = pl.ds(pl.multiple_of(oc * half, 128), half)
+    here = pl.ds(pl.multiple_of(c * half, 128), half)
+    n_rows = 2
+    tall = count // n_rows
+    down = []
+    for r in range(n_rows):
+        rows = slice(r * tall, (r + 1) * tall)
+        downb[r] = jnp.dot(hid[rows, :], wd[:, there], preferred_element_type=F32).astype(BF)
+        copy = remote(downb.at[r], downr.at[r], s_dn.at[r], r_dn.at[r], partner)
+        copy.start()
+        down.append(copy)
+    for r in range(n_rows):
+        rows = slice(r * tall, (r + 1) * tall)
+        mine = jnp.dot(hid[rows, :], wd[:, here], preferred_element_type=F32)
+        down[r].wait_recv()
+        mine = mine + downr[r].astype(F32)
+        a0, a1, b = mine[:, :128], mine[:, 128:256], mine[:, 256:384]
+        total = jnp.concatenate([a0, b[:, :64], a1, b[:, 64:]], 1) + first[rows, here]
+        out[rows, :] = total.astype(BF)
+    for copy in down + sends:
+        copy.wait_send()
+
+
+def on_device_fused(sizes, tokens, norm1_gain, w_qkv, w_out, norm2_gain, w_up, w_down):
+    n_g, n_ha, n_ta = sizes
+    frames, rows_h, width, half = tokens.shape
+    lines = frames * rows_h
+    count = lines * width
+    strips = n_ha * n_ta
+    narrow = width // strips
+    same = rows_h * narrow
+    units = w_up.shape[1]
+    packed = units // 4 * 3 // 2
+    dma = pltpu.SemaphoreType.DMA
+    vm = pltpu.VMEM
+    n_moves = strips - 1
+    scratch = [
+        vm((2, lines, width, half), BF),
+        vm((strips, lines * narrow, half), BF),
+        vm((2, strips, lines * narrow, half), BF),
+        vm((count, 2 * half), BF),
+        vm((3, n_ta, n_ha, frames, same, half), BF),
+        vm((n_ta, n_ha, frames, same, half), F32),
+        vm((count // 128, 128, half), F32),
+        vm((n_ta, n_ha, frames, same, half), BF),
+        vm((n_ta, n_ha, frames, same, half), BF),
+        vm((2, count, half), BF),
+        vm((count, 2 * half), F32),
+        vm((3, 2 * half, half), BF),
+        vm((2, half, 2 * half), BF),
+        vm((n_ha, 4, w_up.shape[0] // 4, units), BF),
+        vm((units, w_down.shape[1]), BF),
+        vm((n_ha, 4, packed, 128), BF),
+        vm((units, 2 * half), BF),
+        vm((count, units), BF),
+        vm((2, count // 2, half), BF),
+        vm((2, count // 2, half), BF),
+        vm((lines, width, half), F32),
+        dma((4,)),
+        dma((n_moves,)), dma((n_moves,)),
+        dma((2,)), dma((2,)),
+        dma((strips,)), dma((strips,)),
+        dma((n_moves,)), dma((n_moves,)),
+        dma((2, n_ha)), dma((2, n_ha)),
+        dma((2, n_ha, 3)), dma((2, n_ha, 3)),
+        dma((1,)), dma((1,)),
+        dma((2,)), dma((2,)),
+    ]
+    in_vmem = pl.BlockSpec(memory_space=pltpu.VMEM)
+    anywhere = pl.BlockSpec(memory_space=pl.ANY)
+    result = pl.pallas_call(
+        functools.partial(block_kernel, sizes),
+        out_shape=jax.ShapeDtypeStruct((count, half), BF),
+        in_specs=[in_vmem, in_vmem, anywhere, anywhere, in_vmem, anywhere, anywhere],
+        out_specs=in_vmem,
+        scratch_shapes=scratch,
+        compiler_params=pltpu.CompilerParams(
+            collective_id=0, has_side_effects=True, vmem_limit_bytes=56 * 2**20
+        ),
+    )(
+        tokens.reshape(lines, width, half), norm1_gain.reshape(1, -1), w_qkv, w_out,
+        norm2_gain.reshape(1, -1), w_up.reshape(4, w_up.shape[0] // 4, units), w_down,
+    )
+    return result.reshape(frames, rows_h, width, half)
+
+
+def fits(mesh):
+    shape = mesh.shape
+    return shape["groups"] == 2 and shape["ta"] == 2 and shape["ha"] == 4 and shape["col"] == 2
+
+
 def solution(mesh):
     placed = (
         P(("groups", "ta"), "ha", None, "col"),
@@ -92,8 +458,11 @@
         P("ha", "col"),
         P("col", "ha"),
     )
+    body = on_device
+    if fits(mesh):
+        body = functools.partial(on_device_fused, (mesh.shape["groups"], mesh.shape["ha"], mesh.shape["ta"]))
     return jax.shard_map(
-        on_device,
+        body,
         mesh=mesh,
         in_specs=placed,
         out_specs=P(("groups", "ta"), "ha", None, "col"),

time: 272 us -> 88.5 us (0.33)
  waiting for transfers between devices: 108 us -> 0 us
  Pallas kernels: 0 us -> 81.7 us
  local copies, waits for them, and re-layouts: 65.5 us -> 6.53 us
  matrix products: 38.2 us -> 0 us
  blocking collectives: 22.7 us -> 0 us
  between operations: 15 us -> 0.01 us
  starting transfers between devices: 14.9 us -> 0 us
  other arithmetic: 6.71 us -> 0 us
    pallas_call x0 -> x1, Pallas kernels: none -> 81.7 us  [on_device_fused(): pl.pallas_call(functools.partial(block_kernel, sizes), out_shape=jax.Shap...]
    all_gather x2 -> x0, waiting for transfers between devices: 78.7 us -> none  [the longest x1 50.3 us: on_device(): lax.all_gather(w_down, 'ha', axis=1, tiled=True)]
    dot_general x9 -> x0, matrix products: 38.2 us -> none  [the longest x1 12.3 us: on_device(): jnp.dot(hidden, lax.all_gather(w_down, 'ha', axis=1, tiled=True), preferr...]
    psum x1 -> x0, waiting for transfers between devices: 20.9 us -> none  [on_device(): summed = lax.psum(terms, 'col')]
    all_to_all x1 -> x0, blocking collectives: 19.9 us -> none  [on_device(): lax.all_to_all(stacked, 'ta', split_axis=3, concat_axis=1, tiled=True)]
    reshape x9 -> x2, local copies, waits for them, and re-layouts: 19 us -> 2.53 us  [the longest x1 1.27 us: on_device_fused(): norm1_gain.reshape(1, -1)]
    convert_element_type x9 -> x0, local copies, waits for them, and re-layouts: 15.1 us -> none  [the longest x2 6.74 us: on_device(): along_w.astype(jnp.float32) + along_h.astype(jnp.float32)]
    all_to_all x3 -> x0, starting transfers between devices: 14.6 us -> none  [the longest x1 5.13 us: on_device(): lax.all_to_all(stacked, 'ha', split_axis=3, concat_axis=2, tiled=True)]
  transfers between devices with their start and end apart: 7 -> 0, of which waited for: 4 -> 0; matrix products, arithmetic and copies ran while one was open for 29% -> 0% of each run, Pallas kernels for 0% -> 0%
where the time goes in v1:
time: 88.5 us; the launch traced here: 88.3 us
  Pallas kernels  81.7 us (92%)
  local copies, waits for them, and re-layouts  6.53 us (7%)
    pallas_call x1, Pallas kernels, on_device_fused(): pl.pallas_call(functools.partial(block_kernel, sizes), out_shape=jax.Shap...  81.7 us
    unnamed x2, local copies, waits for them, and re-layouts  3.99 us

profile of v1, /device:TPU:0, one launch (start us, length us, event | category | flops | bytes accessed | tf_op | source)
XLA Modules:
  0.0 88.3 jit_solution(14596728915402467769)
XLA Ops:
  0.0 1.3 %reshape.16.gain1 = f32[1,768]{1,0:T(1,128)} reshape(f32[768]{0:T(1024)} %param.8) | data formatting | bytes 6144 | tf_op jit(solution)/shard_map/reshape | solution.py:440
  1.3 1.3 %reshape.17.gain2 = f32[1,768]{1,0:T(1,128)} reshape(f32[768]{0:T(1024)} %param.11) | data formatting | bytes 6144 | tf_op jit(solution)/shard_map/reshape | solution.py:441
  2.5 2.2 %copy.8.wdn_hbm = bf16[1536,192]{1,0:T(8,128)(2,1)} copy(bf16[1536,192]{0,1:T(8,128)(2,1)} %param.13) | data formatting | bytes 1179648 | tf_op args[6]
  4.7 81.7 %shard_map.73 = bf16[512,384]{1,0:T(8,128)(2,1)} custom-call(bf16[8,64,384]{2,1,0:T(8,128)(2,1)} %bitcast.5, f32[1,768]{1,0:T(1,128)} %reshape.16.gain1, bf16[3,768,384]{2,1,0:T(8,128)(2,1)} %wqkv_hbm.1, bf16[384,768]{1,0:T(8,128)(2,1)} %wout_hbm.1, f32[1,768]{1,0:T(1,128)} %reshape.17.gain2, bf16[4,48,1536]{2,1,0:T(8,128)(2,1)} %bitcast.4, ...), custom_call_target="tpu_custom_call" | custom-call | tf_op jit(solution)/shard_map/pallas_call | solution.py:430
  86.5 1.8 %copy.10 = bf16[2,4,64,384]{3,2,1,0:T(8,128)(2,1)} copy(bf16[2,4,64,384]{3,2,1,0:T(8,128)(2,1)} %bitcast.3) | data formatting | bytes 786432

commit v2 on v1

--- a/solution.py
+++ b/solution.py
@@ -98,7 +98,7 @@
     spread = sum(jnp.sum(part * part, -1, keepdims=True) for part in centred) * (1.0 / model)
     factor = lax.rsqrt(spread + EPS)
     for at, part in enumerate(centred):
-        gain = gain_ref[:, at * half : (at + 1) * half]
+        gain = gain_ref[at * half : (at + 1) * half].reshape(1, half)
         out_ref[rows, at * half : (at + 1) * half] = (part * factor * gain).astype(BF)
 
 
@@ -119,7 +119,7 @@
 def block_kernel(
     sizes, tok, gain1, wqkv_hbm, wout_hbm, gain2, wup_hbm, wdn_hbm, out,
     own, sendb, strip, nrm, qkv, found, heads_w, backb, back, mix, first,
-    wq, wo, wu, wdl, wdp, wd, hid, downb, downr, wide,
+    wq, wo, wu, wd, hid, downb, downr, wide,
     sem_l, s_tok, r_tok, s_col, r_col, s_fwd, r_fwd, s_ret, r_ret,
     s_z, r_z, s_p, r_p, s_mix, r_mix, s_dn, r_dn,
 ):
@@ -154,7 +154,7 @@
             pl.semaphore_signal(barrier, inc=1, device_id=to, device_id_type=pl.DeviceIdType.MESH)
 
     local = [
-        pltpu.make_async_copy(wdn_hbm, wdl, sem_l.at[0]),
+        pltpu.make_async_copy(wdn_hbm, wd.at[z], sem_l.at[0]),
         pltpu.make_async_copy(wqkv_hbm, wq, sem_l.at[1]),
         pltpu.make_async_copy(wout_hbm, wo.at[c], sem_l.at[2]),
         pltpu.make_async_copy(wup_hbm, wu.at[z], sem_l.at[3]),
@@ -186,29 +186,82 @@
     forward.start()
     sends.append(forward)
 
-    z_up, z_down = [], []
-    local[0].wait()
-    part_rows = wdl.shape[0] // 4
-    for q in range(4):
-        piece = wdl[q * part_rows : (q + 1) * part_rows, :].astype(F32)
-        wdp[z, q, :part_rows] = piece[:, :128].astype(BF)
-        rest = piece[:, 128:]
-        wdp[z, q, part_rows:] = jnp.concatenate([rest[: part_rows // 2], rest[part_rows // 2 :]], 1).astype(BF)
-    for d in range(1, n_ha):
-        to = {"ha": lax.rem(z + d, n_ha)}
-        copy = remote(wup_hbm.at[quarter], wu.at[z, quarter], s_z.at[0, d], r_z.at[0, d], to)
-        copy.start()
-        z_up.append(copy)
-    for d in range(1, n_ha):
-        to = {"ha": lax.rem(z + d, n_ha)}
-        copy = remote(wdp.at[z, quarter], wdp.at[z, quarter], s_z.at[1, d], r_z.at[1, d], to)
-        copy.start()
-        z_down.append(copy)
+    held, given = (wu, wd), (wup_hbm, wdn_hbm)
+    when_sends = []
+    near = [{"groups": lax.rem(g + 1, n_g)}, {"ta": lax.rem(t + 1, n_ta)}]
+
+    def line_copy(kind, way, k, shard):
+        at = 0 if way > 0 else 1
+        source = given[kind].at[quarter] if k == 1 else held[kind].at[shard, quarter]
+        to = {"ha": lax.rem(z + way + n_ha, n_ha)}
+        return remote(source, held[kind].at[shard, quarter], s_z.at[kind, at, k - 1], r_z.at[kind, at, k - 1], to)
+
+    def plane_copy(kind, shard, at):
+        sides = near if kind == 0 else near[::-1]
+        flip_g = lax.rem(g + 1, n_g) + t * n_g
+        flip_t = lax.rem(t + 1, n_ta) * n_g + g
+        theirs = flip_g if kind == 0 else flip_t
+        piece = held[kind].at[shard, theirs if at == 2 else quarter]
+        return remote(piece, piece, s_p.at[kind, shard, at], r_p.at[kind, shard, at], sides[min(at, 1)])
+
+    def plane_landing(kind, shard, at):
+        flip_g = lax.rem(g + 1, n_g) + t * n_g
+        flip_t = lax.rem(t + 1, n_ta) * n_g + g
+        flip_both = lax.rem(t + 1, n_ta) * n_g + lax.rem(g + 1, n_g)
+        first_of = (flip_g, flip_t, flip_both) if kind == 0 else (flip_t, flip_g, flip_both)
+        piece = held[kind].at[shard, first_of[at]]
+        return remote(piece, piece, s_p.at[kind, shard, at], r_p.at[kind, shard, at], near[0])
+
+    def starts_when(cond, copy):
+        @pl.when(cond)
+        def _():
+            copy.start()
+
+        when_sends.append((cond, copy))
+
+    def line_first(kind):
+        for way in (1, -1):
+            ahead = z + way
+            starts_when((ahead >= 0) & (ahead < n_ha), line_copy(kind, way, 1, z))
+
+    def line_step(kind, k):
+        for way in (1, -1):
+            shard = z - way * k
+            ahead = z + way
+            here = (shard >= 0) & (shard < n_ha)
+            safe = lax.rem(shard + n_ha, n_ha)
+            landing = held[kind].at[safe, quarter]
+            at = 0 if way > 0 else 1
+
+            @pl.when(here)
+            def _():
+                remote(landing, landing, s_z.at[kind, at, k - 1], r_z.at[kind, at, k - 1], partner).wait_recv()
+
+            if k < n_ha - 1:
+                starts_when(here & (ahead >= 0) & (ahead < n_ha), line_copy(kind, way, k + 1, safe))
+            for side in range(2):
+                starts_when(here, plane_copy(kind, safe, side))
+
+    def plane_step(kind):
+        for d in range(1, n_ha):
+            shard = lax.rem(z + d, n_ha)
+            plane_landing(kind, shard, 0).wait_recv()
+            copy = plane_copy(kind, shard, 2)
+            copy.start()
+            sends.append(copy)
+
+    def plane_wait(kind):
+        for d in range(1, n_ha):
+            shard = lax.rem(z + d, n_ha)
+            plane_landing(kind, shard, 1).wait_recv()
+            plane_landing(kind, shard, 2).wait_recv()
+
+    line_first(0)
+    line_first(1)
     local[1].wait()
     local[2].wait()
     wo_send = remote(wo.at[c], wo.at[c], s_col.at[1], r_col.at[1], partner)
     wo_send.start()
-    sends += z_up + z_down
 
     def project():
         for i in range(3):
@@ -252,11 +305,13 @@
         from_t, from_z = lax.rem(t + n_ta - dt, n_ta), lax.rem(z + n_ha - dz, n_ha)
         src = from_t * n_ha + from_z
         remote(strip.at[oc, src], strip.at[oc, src], s_fwd.at[at], r_fwd.at[at], partner).wait_recv()
+    line_step(0, 1)
     norm_rows(
         [strip[0].reshape(count, half).astype(F32), strip[1].reshape(count, half).astype(F32)],
         gain1, nrm, slice(None),
     )
     project()
+    line_step(0, 2)
     frames = 2
     mask_h = lax.rem(rows_at, narrow) == lax.rem(cols_at, narrow)
     same = lines // frames * narrow
@@ -279,6 +334,8 @@
         return carry
 
     lax.fori_loop(0, n_ta * frames, along_h, 0)
+    line_step(1, 1)
+    line_step(0, 3)
     lax.fori_loop(0, n_ha, along_t, 0)
 
     for at, (dt, dz) in enumerate(moves):
@@ -288,25 +345,8 @@
         sends.append(copy)
     back[t, z] = backb[t, z]
 
-    def spread(kind, buf):
-        for d in range(1, n_ha):
-            zz = lax.rem(z + n_ha - d, n_ha)
-            remote(buf.at[zz, quarter], buf.at[zz, quarter], s_z.at[kind, d], r_z.at[kind, d], partner).wait_recv()
-            for at, (dt, dg) in enumerate(plane):
-                to = {"groups": lax.rem(g + dg, n_g), "ta": lax.rem(t + dt, n_ta)}
-                copy = remote(buf.at[zz, quarter], buf.at[zz, quarter], s_p.at[kind, d, at], r_p.at[kind, d, at], to)
-                copy.start()
-                sends.append(copy)
-
-    def spread_wait(kind, buf):
-        for d in range(1, n_ha):
-            zz = lax.rem(z + n_ha - d, n_ha)
-            for at, (dt, dg) in enumerate(plane):
-                qq = lax.rem(t + n_ta - dt, n_ta) * n_g + lax.rem(g + n_g - dg, n_g)
-                remote(buf.at[zz, qq], buf.at[zz, qq], s_p.at[kind, d, at], r_p.at[kind, d, at], partner).wait_recv()
-
-    spread(0, wu)
-
+    line_step(1, 2)
+    plane_step(0)
     for at, (dt, dz) in enumerate(moves):
         from_t, from_z = lax.rem(t + n_ta - dt, n_ta), lax.rem(z + n_ha - dz, n_ha)
         remote(back.at[from_t, from_z], back.at[from_t, from_z], s_ret.at[at], r_ret.at[at], partner).wait_recv()
@@ -316,7 +356,7 @@
     mix[c] = (wide[...].reshape(count, half) + heads_w[...].reshape(count, half)).astype(BF)
     mix_send = remote(mix.at[c], mix.at[c], s_mix.at[0], r_mix.at[0], partner)
     mix_send.start()
-    spread(1, wdp)
+    line_step(1, 3)
     wo_send.wait()
     first[...] = jnp.dot(mix[c], wo[c], preferred_element_type=F32)
     mix_send.wait()
@@ -329,8 +369,9 @@
         parts.append(part)
     norm_rows(parts, gain2, nrm, slice(None))
 
+    plane_step(1)
     local[3].wait()
-    spread_wait(0, wu)
+    plane_wait(0)
     units = wu.shape[3]
     step = 256
 
@@ -343,41 +384,37 @@
 
     lax.fori_loop(0, units // step, feed, 0)
 
-    spread_wait(1, wdp)
-    small = part_rows // 2
-    low = lax.broadcasted_iota(jnp.int32, (small, 128), 1) < 64
-    for q in range(4):
-        for zp in range(n_ha // 2):
-            lead = zp * 384
-            rows = slice(q * part_rows, (q + 1) * part_rows)
-            wd[rows, lead : lead + 128] = wdp[2 * zp, q, :part_rows]
-            wd[rows, lead + 128 : lead + 256] = wdp[2 * zp + 1, q, :part_rows]
-            even = wdp[2 * zp, q, part_rows:].astype(F32)
-            odd = wdp[2 * zp + 1, q, part_rows:].astype(F32)
-            wd[q * part_rows : q * part_rows + small, lead + 256 : lead + 384] = jnp.where(low, even, pltpu.roll(odd, 64, 1)).astype(BF)
-            wd[q * part_rows + small : (q + 1) * part_rows, lead + 256 : lead + 384] = jnp.where(low, pltpu.roll(even, 64, 1), odd).astype(BF)
-
-    there = pl.ds(pl.multiple_of(oc * half, 128), half)
+    local[0].wait()
+    plane_wait(1)
     here = pl.ds(pl.multiple_of(c * half, 128), half)
+    share = n_ha // 2
+
+    def down_dot(rows, side):
+        weights = wd[pl.ds(side * share, share)].reshape(half, units)
+        return lax.dot_general(hid[rows, :], weights, (((1,), (1,)), ((), ())), preferred_element_type=F32)
+
     n_rows = 2
     tall = count // n_rows
     down = []
     for r in range(n_rows):
         rows = slice(r * tall, (r + 1) * tall)
-        downb[r] = jnp.dot(hid[rows, :], wd[:, there], preferred_element_type=F32).astype(BF)
+        downb[r] = down_dot(rows, oc).astype(BF)
         copy = remote(downb.at[r], downr.at[r], s_dn.at[r], r_dn.at[r], partner)
         copy.start()
         down.append(copy)
     for r in range(n_rows):
         rows = slice(r * tall, (r + 1) * tall)
-        mine = jnp.dot(hid[rows, :], wd[:, here], preferred_element_type=F32)
+        mine = down_dot(rows, c)
         down[r].wait_recv()
         mine = mine + downr[r].astype(F32)
-        a0, a1, b = mine[:, :128], mine[:, 128:256], mine[:, 256:384]
-        total = jnp.concatenate([a0, b[:, :64], a1, b[:, 64:]], 1) + first[rows, here]
-        out[rows, :] = total.astype(BF)
+        out[rows, :] = (mine + first[rows, here]).astype(BF)
     for copy in down + sends:
         copy.wait_send()
+    for cond, copy in when_sends:
+
+        @pl.when(cond)
+        def _():
+            copy.wait_send()
 
 
 def on_device_fused(sizes, tokens, norm1_gain, w_qkv, w_out, norm2_gain, w_up, w_down):
@@ -389,7 +426,6 @@
     narrow = width // strips
     same = rows_h * narrow
     units = w_up.shape[1]
-    packed = units // 4 * 3 // 2
     dma = pltpu.SemaphoreType.DMA
     vm = pltpu.VMEM
     n_moves = strips - 1
@@ -408,9 +444,7 @@
         vm((3, 2 * half, half), BF),
         vm((2, half, 2 * half), BF),
         vm((n_ha, 4, w_up.shape[0] // 4, units), BF),
-        vm((units, w_down.shape[1]), BF),
-        vm((n_ha, 4, packed, 128), BF),
-        vm((units, 2 * half), BF),
+        vm((n_ha, 4, w_up.shape[0] // 4, units), BF),
         vm((count, units), BF),
         vm((2, count // 2, half), BF),
         vm((2, count // 2, half), BF),
@@ -420,7 +454,7 @@
         dma((2,)), dma((2,)),
         dma((strips,)), dma((strips,)),
         dma((n_moves,)), dma((n_moves,)),
-        dma((2, n_ha)), dma((2, n_ha)),
+        dma((2, 2, n_ha)), dma((2, 2, n_ha)),
         dma((2, n_ha, 3)), dma((2, n_ha, 3)),
         dma((1,)), dma((1,)),
         dma((2,)), dma((2,)),
@@ -437,8 +471,9 @@
             collective_id=0, has_side_effects=True, vmem_limit_bytes=56 * 2**20
         ),
     )(
-        tokens.reshape(lines, width, half), norm1_gain.reshape(1, -1), w_qkv, w_out,
-        norm2_gain.reshape(1, -1), w_up.reshape(4, w_up.shape[0] // 4, units), w_down,
+        tokens.reshape(lines, width, half), norm1_gain, w_qkv, w_out,
+        norm2_gain, w_up.reshape(4, w_up.shape[0] // 4, units),
+        w_down.T.reshape(4, w_up.shape[0] // 4, units),
     )
     return result.reshape(frames, rows_h, width, half)
 

time: 88.5 us -> 69.4 us (0.78)
  the two profiles are of different devices: /device:TPU:0 before, /device:TPU:25 now
where the time goes in v2:
time: 69.4 us; the launch traced here: 69.2 us
  Pallas kernels  67.4 us (97%)
  local copies, waits for them, and re-layouts  1.78 us (3%)
    pallas_call x1, Pallas kernels, on_device_fused(): pl.pallas_call(functools.partial(block_kernel, sizes), out_shape=jax.Shap...  67.4 us
    unnamed x1, local copies, waits for them, and re-layouts  1.78 us

profile of v2, /device:TPU:25, one launch (start us, length us, event | category | flops | bytes accessed | tf_op | source)
XLA Modules:
  0.0 69.2 jit_solution(2012865155581216740)
XLA Ops:
  0.0 67.4 %shard_map.73 = bf16[512,384]{1,0:T(8,128)(2,1)} custom-call(bf16[8,64,384]{2,1,0:T(8,128)(2,1)} %bitcast.9, f32[768]{0:T(1024)} %gain1.1, bf16[3,768,384]{2,1,0:T(8,128)(2,1)} %wqkv_hbm.1, bf16[384,768]{1,0:T(8,128)(2,1)} %wout_hbm.1, f32[768]{0:T(1024)} %gain2.1, bf16[4,48,1536]{2,1,0:T(8,128)(2,1)} %bitcast.7, bf16[4,48,1536]{2,1,0:T(8,128)(2,1)} %bitcast.8), custom_call_target="tpu_custom_call" | custom-call | tf_op jit(solution)/shard_map/pallas_call | solution.py:464
  67.4 1.8 %copy.9 = bf16[2,4,64,384]{3,2,1,0:T(8,128)(2,1)} copy(bf16[2,4,64,384]{3,2,1,0:T(8,128)(2,1)} %bitcast.6) | data formatting | bytes 786432

commit v3 on v2

--- a/solution.py
+++ b/solution.py
@@ -242,13 +242,18 @@
             for side in range(2):
                 starts_when(here, plane_copy(kind, safe, side))
 
-    def plane_step(kind):
-        for d in range(1, n_ha):
-            shard = lax.rem(z + d, n_ha)
-            plane_landing(kind, shard, 0).wait_recv()
-            copy = plane_copy(kind, shard, 2)
-            copy.start()
-            sends.append(copy)
+    def plane_step(kind, k):
+        for way in (1, -1):
+            shard = z - way * k
+            here = (shard >= 0) & (shard < n_ha)
+            safe = lax.rem(shard + n_ha, n_ha)
+            landing = plane_landing(kind, safe, 0)
+
+            @pl.when(here)
+            def _():
+                landing.wait_recv()
+
+            starts_when(here, plane_copy(kind, safe, 2))
 
     def plane_wait(kind):
         for d in range(1, n_ha):
@@ -257,7 +262,6 @@
             plane_landing(kind, shard, 2).wait_recv()
 
     line_first(0)
-    line_first(1)
     local[1].wait()
     local[2].wait()
     wo_send = remote(wo.at[c], wo.at[c], s_col.at[1], r_col.at[1], partner)
@@ -282,6 +286,7 @@
         gain1, nrm, slice(None),
     )
     project()
+    line_first(1)
     width = tok.shape[1]
     mask_w = rows_at // width == cols_at // width
     flat = qkv.reshape(3, count // block, block, half)
@@ -292,7 +297,8 @@
             heads_w[b, :, lanes] = attend_pair(flat[0, b, :, lanes], flat[1, b, :, lanes], flat[2, b, :, lanes], mask_w)
         return carry
 
-    lax.fori_loop(0, count // block, along_w, 0)
+    lax.fori_loop(0, count // block, along_w, 0, unroll=2)
+    line_step(0, 1)
 
     for at, (dt, dz) in enumerate(moves):
         from_t, from_z = lax.rem(t + n_ta - dt, n_ta), lax.rem(z + n_ha - dz, n_ha)
@@ -305,13 +311,14 @@
         from_t, from_z = lax.rem(t + n_ta - dt, n_ta), lax.rem(z + n_ha - dz, n_ha)
         src = from_t * n_ha + from_z
         remote(strip.at[oc, src], strip.at[oc, src], s_fwd.at[at], r_fwd.at[at], partner).wait_recv()
-    line_step(0, 1)
+    line_step(1, 1)
     norm_rows(
         [strip[0].reshape(count, half).astype(F32), strip[1].reshape(count, half).astype(F32)],
         gain1, nrm, slice(None),
     )
     project()
     line_step(0, 2)
+    plane_step(0, 1)
     frames = 2
     mask_h = lax.rem(rows_at, narrow) == lax.rem(cols_at, narrow)
     same = lines // frames * narrow
@@ -333,10 +340,11 @@
             backb[:, zz, :, :, lanes] = (found[:, zz, :, :, lanes] + more).astype(BF)
         return carry
 
-    lax.fori_loop(0, n_ta * frames, along_h, 0)
-    line_step(1, 1)
+    lax.fori_loop(0, n_ta * frames, along_h, 0, unroll=2)
+    line_step(1, 2)
+    plane_step(1, 1)
     line_step(0, 3)
-    lax.fori_loop(0, n_ha, along_t, 0)
+    lax.fori_loop(0, n_ha, along_t, 0, unroll=2)
 
     for at, (dt, dz) in enumerate(moves):
         to_t, to_z = other(dt, dz)
@@ -344,9 +352,10 @@
         copy.start()
         sends.append(copy)
     back[t, z] = backb[t, z]
-
-    line_step(1, 2)
-    plane_step(0)
+    line_step(1, 3)
+    plane_step(0, 2)
+    plane_step(0, 3)
+
     for at, (dt, dz) in enumerate(moves):
         from_t, from_z = lax.rem(t + n_ta - dt, n_ta), lax.rem(z + n_ha - dz, n_ha)
         remote(back.at[from_t, from_z], back.at[from_t, from_z], s_ret.at[at], r_ret.at[at], partner).wait_recv()
@@ -356,7 +365,7 @@
     mix[c] = (wide[...].reshape(count, half) + heads_w[...].reshape(count, half)).astype(BF)
     mix_send = remote(mix.at[c], mix.at[c], s_mix.at[0], r_mix.at[0], partner)
     mix_send.start()
-    line_step(1, 3)
+    plane_step(1, 2)
     wo_send.wait()
     first[...] = jnp.dot(mix[c], wo[c], preferred_element_type=F32)
     mix_send.wait()
@@ -369,8 +378,8 @@
         parts.append(part)
     norm_rows(parts, gain2, nrm, slice(None))
 
-    plane_step(1)
     local[3].wait()
+    plane_step(1, 3)
     plane_wait(0)
     units = wu.shape[3]
     step = 256
@@ -382,10 +391,11 @@
         hid[:, cols] = up.astype(BF)
         return carry
 
-    lax.fori_loop(0, units // step, feed, 0)
+    lax.fori_loop(0, 3, feed, 0)
+    lax.fori_loop(3, units // step, feed, 0)
+    plane_wait(1)
 
     local[0].wait()
-    plane_wait(1)
     here = pl.ds(pl.multiple_of(c * half, 128), half)
     share = n_ha // 2
 

time: 69.4 us -> 60.7 us (0.87)
  the two profiles are of different devices: /device:TPU:25 before, /device:TPU:0 now
where the time goes in v3:
time: 60.7 us; the launch traced here: 59.9 us
  Pallas kernels  58.1 us (96%)
  local copies, waits for them, and re-layouts  1.78 us (3%)
    pallas_call x1, Pallas kernels, on_device_fused(): pl.pallas_call(functools.partial(block_kernel, sizes), out_shape=jax.Shap...  58.1 us
    unnamed x1, local copies, waits for them, and re-layouts  1.78 us

profile of v3, /device:TPU:0, one launch (start us, length us, event | category | flops | bytes accessed | tf_op | source)
XLA Modules:
  0.0 59.9 jit_solution(6265559108479804304)
XLA Ops:
  0.0 58.1 %shard_map.73 = bf16[512,384]{1,0:T(8,128)(2,1)} custom-call(bf16[8,64,384]{2,1,0:T(8,128)(2,1)} %bitcast.9, f32[768]{0:T(1024)} %gain1.1, bf16[3,768,384]{2,1,0:T(8,128)(2,1)} %wqkv_hbm.1, bf16[384,768]{1,0:T(8,128)(2,1)} %wout_hbm.1, f32[768]{0:T(1024)} %gain2.1, bf16[4,48,1536]{2,1,0:T(8,128)(2,1)} %bitcast.7, bf16[4,48,1536]{2,1,0:T(8,128)(2,1)} %bitcast.8), custom_call_target="tpu_custom_call" | custom-call | tf_op jit(solution)/shard_map/pallas_call | solution.py:474
  58.1 1.8 %copy.9 = bf16[2,4,64,384]{3,2,1,0:T(8,128)(2,1)} copy(bf16[2,4,64,384]{3,2,1,0:T(8,128)(2,1)} %bitcast.6) | data formatting | bytes 786432
